TPU v7x, 512 devices: a whole 4x8x8 slice. The times are simulated.
512 devices in a mesh: section: 8 (over y_hi, x), dp: 64 (over y_lo, z, core).
Axes of the slice: x: 4, y: 8 (y_hi: 2, y_lo: 4; y = y_hi * 4 + y_lo), z: 8, core: 2. Of those that a mesh axis runs over, the one named last changes fastest.
Arguments:
- embeds: bfloat16 [12288, 3584], P('dp'), may hold values from -16 to 16
- cotangent: bfloat16 [12288, 3584], P('dp'), may hold values from -1 to 1
- adapter_a: bfloat16 [8, 7168, 128], P('section', 'dp'), may hold values from -0.0625 to 0.0625
- adapter_b: bfloat16 [8, 128, 3584], P('section', None, 'dp'), may hold values from -0.5 to 0.5
- norm_gains: float32 [2, 7168], replicated, may hold values from 0.5 to 1.5
Outputs:
- grad_a: float32 [8, 7168, 128], P('section', 'dp')
- grad_b: float32 [8, 128, 3584], P('section')
- grad_gain: float32 [2, 7168], P(None, 'dp')
- grad_embed: bfloat16 [12288, 3584], P('dp', 'section')
All inputs are finite; a program needn't handle non-finite values.
Results may differ from a plain program's by a relative error of at most 0.023.
Values may be sent and summed in bfloat16 or wider, within the bound.
A program may use at most 64 MiB of HBM per device.

v0:
```python
import jax
import jax.numpy as jnp
from jax import lax
from jax.sharding import PartitionSpec as P

MROWS = 24
epsilon = 1e-05


def from_behind(block, axis, distance):
    devices = range(lax.axis_size(axis))
    route = [(i - distance, i) for i in devices if i - distance in devices]
    return lax.ppermute(block, axis, route)


def normalize(hidden, embeds, gain_row):
    joined = jnp.concatenate([hidden.astype(jnp.float32), embeds.astype(jnp.float32)], axis=1)
    inv_rms = lax.rsqrt(jnp.mean(joined * joined, axis=1, keepdims=True) + epsilon)
    normed = joined * inv_rms
    lowered = (normed * gain_row[None, :]).astype(jnp.bfloat16)
    return (normed, inv_rms, lowered)


def contract(left_op, right_op, left_dim, right_dim):
    return lax.dot_general(
        left_op,
        right_op,
        (((left_dim,), (right_dim,)), ((), ())),
        preferred_element_type=jnp.float32,
    )


def pass_on(payload, offset):
    return from_behind(payload, "section", offset)


def pick(stacked, index):
    return lax.dynamic_index_in_dim(stacked, index, 0, keepdims=False)


def place(stacked, index, value, active):
    current = pick(stacked, index)
    return lax.dynamic_update_index_in_dim(stacked, jnp.where(active, value, current), index, 0)


def per_device(embeds, cotangent, adapter_a, adapter_b, norm_gains):
    sections = lax.axis_size("section")
    section_id = lax.axis_index("section")
    down_mat, up_mat = (
        lax.all_gather(adapter_a[0], "dp", axis=0, tiled=True),
        lax.all_gather(adapter_b[0], "dp", axis=1, tiled=True),
    )
    parity = section_id % 2
    gain_row = jnp.where(parity == 0, norm_gains[0], norm_gains[1])
    model_width = embeds.shape[1]
    joined_width = down_mat.shape[0]
    low_rank = down_mat.shape[1]
    group_size = 1
    block_rows = MROWS * group_size
    block_count = embeds.shape[0] // block_rows
    tick_count = block_count + sections - 1
    embed_blocks = embeds.reshape(block_count, block_rows, model_width)
    target_blocks = cotangent.reshape(block_count, block_rows, model_width)

    def forward_tick(tick, state_in):
        incoming, hidden_keep, reduced_keep = state_in
        block_index = tick - section_id
        active = (block_index >= 0) & (block_index < block_count)
        safe_index = jnp.clip(block_index, 0, block_count - 1)
        embed_block = pick(embed_blocks, safe_index)
        hidden = jnp.where(section_id == 0, embed_block, incoming)
        normed, inv_rms, lowered = normalize(hidden, embed_block, gain_row)
        reduced = jnp.dot(lowered, down_mat, preferred_element_type=jnp.float32).astype(
            jnp.bfloat16
        )
        output = (
            hidden.astype(jnp.float32)
            + jnp.dot(reduced, up_mat, preferred_element_type=jnp.float32)
        ).astype(jnp.bfloat16)
        hidden_keep = place(hidden_keep, safe_index, hidden, active)
        reduced_keep = place(reduced_keep, safe_index, reduced, active)
        outgoing = jnp.where(active, output, jnp.zeros_like(output))
        return (pass_on(outgoing, 1), hidden_keep, reduced_keep)

    forward_init = (
        jnp.zeros((block_rows, model_width), jnp.bfloat16),
        jnp.zeros((block_count, block_rows, model_width), jnp.bfloat16),
        jnp.zeros((block_count, block_rows, low_rank), jnp.bfloat16),
    )
    last_sent, hidden_keep, reduced_keep = lax.fori_loop(0, tick_count, forward_tick, forward_init)

    def backward_tick(tick, state_in):
        incoming, grad_a, grad_b, gain_acc, term_keep = state_in
        block_index = tick - (sections - 1 - section_id)
        active = (block_index >= 0) & (block_index < block_count)
        safe_index = jnp.clip(block_index, 0, block_count - 1)
        target = pick(target_blocks, safe_index)
        back_in = jnp.where(section_id == sections - 1, target, incoming)
        back_in = jnp.where(active, back_in, jnp.zeros_like(back_in))
        hidden = pick(hidden_keep, safe_index)
        reduced = pick(reduced_keep, safe_index)
        embed_block = pick(embed_blocks, safe_index)
        normed, inv_rms, lowered = normalize(hidden, embed_block, gain_row)
        up_grad = contract(back_in, up_mat, 1, 1).astype(jnp.bfloat16)
        grad_b = grad_b + contract(reduced, back_in, 0, 0)
        grad_lowered = contract(up_grad, down_mat, 1, 1)
        grad_a = grad_a + contract(lowered, up_grad, 0, 0)
        gain_acc = gain_acc + jnp.sum(grad_lowered * normed, axis=0)
        scaled = grad_lowered * gain_row[None, :]
        grad_joined = inv_rms * (scaled - normed * jnp.mean(scaled * normed, axis=1, keepdims=True))
        back_out = (back_in.astype(jnp.float32) + grad_joined[:, :model_width]).astype(jnp.bfloat16)
        embed_tail = grad_joined[:, model_width:] + jnp.where(
            section_id == 0, back_out.astype(jnp.float32), 0.0
        )
        term_keep = place(term_keep, safe_index, embed_tail.astype(jnp.bfloat16), active)
        return (pass_on(back_out, -1), grad_a, grad_b, gain_acc, term_keep)

    backward_init = (
        jnp.zeros((block_rows, model_width), jnp.bfloat16),
        jnp.zeros((joined_width, low_rank), jnp.float32),
        jnp.zeros((low_rank, model_width), jnp.float32),
        jnp.zeros((joined_width,), jnp.float32),
        jnp.zeros((block_count, block_rows, model_width), jnp.bfloat16),
    )
    last_back, grad_a, grad_b, gain_acc, term_keep = lax.fori_loop(
        0, tick_count, backward_tick, backward_init
    )
    gain_pair = jnp.stack(
        [jnp.where(parity == 0, gain_acc, 0.0), jnp.where(parity == 1, gain_acc, 0.0)]
    )
    grad_a_part, gain_part = (
        lax.psum_scatter(grad_a, "dp", scatter_dimension=0, tiled=True),
        lax.psum_scatter(gain_pair, "dp", scatter_dimension=1, tiled=True),
    )
    grad_b_sum = lax.psum(grad_b, "dp")
    embed_terms = term_keep.reshape(-1, model_width).astype(jnp.float32)
    embed_sum, gain_sum = (
        lax.psum(embed_terms.astype(jnp.bfloat16), "section").astype(jnp.float32),
        lax.psum(gain_part.astype(jnp.bfloat16), "section").astype(jnp.float32),
    )
    column_count = model_width // sections
    embed_cols = lax.dynamic_slice_in_dim(embed_sum, section_id * column_count, column_count, 1)
    return (grad_a_part[None], grad_b_sum[None], gain_sum, embed_cols.astype(jnp.bfloat16))


def solution(mesh):
    in_specs = (
        P("dp", None),
        P("dp", None),
        P("section", "dp", None),
        P("section", None, "dp"),
        P(),
    )
    out_specs = (
        P("section", "dp", None),
        P("section", None, None),
        P(None, "dp"),
        P("dp", "section"),
    )
    return jax.shard_map(
        per_device, mesh=mesh, in_specs=in_specs, out_specs=out_specs, check_vma=False
    )
```

profile of v0, /device:TPU:2, one launch (start us, length us, event | category | flops | bytes accessed | tf_op | source)
XLA Modules:
  0.0 1952.0 jit_solution(14938094379765959038)
XLA Ops:
  8.0 88.9 %all-gather.1 = bf16[1,128,3584]{1,2,0:T(8,128)(2,1)S(1)} all-gather(bf16[1,128,56]{1,2,0:T(8,128)(2,1)} %param.12), channel_id=3, replica_groups=mesh['section'=8,'dp'=64] {'dp'}, dimensions={2}, use_global_device_ids=true | all-gather | bytes 931840 | tf_op jit(solution)/shard_map/all_gather | solution.py:51
  97.4 34.4 %all-gather.4.cloned.1.call-done = bf16[1,7168,128]{2,1,0:T(8,128)(2,1)} async-done(((bf16[1,112,128]{2,1,0:T(8,128)(2,1)}), bf16[1,7168,128]{2,1,0:T(8,128)(2,1)}) %all-gather.4.cloned.1.call-update) | async-done | bytes 1835024 | tf_op jit(solution)/shard_map/all_gather | solution.py:50
  133.7 259.5 %while.42 = (s32[]{:T(128)}, bf16[24,3584]{1,0:T(8,128)(2,1)S(1)}, bf16[8,24,3584]{2,1,0:T(8,128)(2,1)}, bf16[8,24,128]{2,1,0:T(8,128)(2,1)}, s32[]{:T(128)}, /*...) while((s32[]{:T(128)}, bf16[24,3584]{1,0:T(8,128)(2,1)S(1)}, ...), condition=%wide.region_2.3_spmd, body=%wide.region_0.2_spmd.sunk | while | flops 67958816 | bytes 14632085 | solution.py:90
  138.7 3.3 collective-permute-start
  142.1 5.1 collective-permute-done
  152.1 3.3 collective-permute-start
  155.4 4.2 collective-permute-done
  164.6 5.0 collective-permute-start
  169.7 2.9 collective-permute-done
  177.5 10.4 collective-permute-start
  195.8 10.5 collective-permute-start
  206.3 2.9 collective-permute-done
  214.2 10.4 collective-permute-start
  224.6 2.9 collective-permute-done
  232.5 10.4 collective-permute-start
  243.0 2.9 collective-permute-done
  250.8 10.5 collective-permute-start
  261.3 2.9 collective-permute-done
  269.2 10.5 collective-permute-start
  287.6 10.5 collective-permute-start
  306.0 10.5 collective-permute-start
  316.5 2.9 collective-permute-done
  324.4 10.5 collective-permute-start
  342.8 10.5 collective-permute-start
  353.3 2.9 collective-permute-done
  361.2 10.5 collective-permute-start
  371.7 2.9 collective-permute-done
  379.5 10.8 collective-permute-start
  390.3 2.9 collective-permute-done
  395.1 308.1 %while.43 = (s32[]{:T(128)}, bf16[24,3584]{1,0:T(8,128)(2,1)}, f32[7168,128]{1,0:T(8,128)}, f32[128,3584]{1,0:T(8,128)}, f32[7168]{0:T(1024)S(1)}, /*index=5*/bf...) while((s32[]{:T(128)}, bf16[24,3584]{1,0:T(8,128)(2,1)}, ...), condition=%wide.region_7.8_spmd.clone, body=%wide.region_3.7_spmd.clone.sunk | while | flops 141248544 | bytes 44095332 | solution.py:125
  406.9 8.3 collective-permute-done.1
  423.8 4.7 convolution_add_fusion.5
  429.9 6.7 collective-permute-done.1
  445.2 4.7 convolution_add_fusion.5
  451.3 8.7 collective-permute-done.1
  468.6 4.7 convolution_add_fusion.5
  474.7 6.4 collective-permute-done.1
  489.6 4.7 convolution_add_fusion.5
  495.7 4.9 collective-permute-done.1
  509.1 4.7 convolution_add_fusion.5
  515.2 5.3 collective-permute-done.1
  529.0 4.7 convolution_add_fusion.5
  535.2 5.5 collective-permute-done.1
  549.3 4.7 convolution_add_fusion.5
  555.4 5.6 collective-permute-done.1
  569.5 4.7 convolution_add_fusion.5
  575.6 5.6 collective-permute-done.1
  589.7 4.7 convolution_add_fusion.5
  595.8 5.6 collective-permute-done.1
  609.9 4.7 convolution_add_fusion.5
  616.1 5.6 collective-permute-done.1
  630.2 4.7 convolution_add_fusion.5
  636.3 5.6 collective-permute-done.1
  650.4 4.7 convolution_add_fusion.5
  656.5 5.6 collective-permute-done.1
  670.6 4.7 convolution_add_fusion.5
  676.7 5.6 collective-permute-done.1
  690.9 4.7 convolution_add_fusion.5
  697.0 5.6 collective-permute-done.1
  707.7 296.9 %reduce-scatter.7.cloned.1.call-done = f32[112,2]{1,0:T(8,128)} async-done(((f32[7168,2]{1,0:T(8,128)}), f32[112,2]{1,0:T(8,128)}) %reduce-scatter.7.cloned.1.call-update) | async-done | bytes 912
  1005.5 24.4 %psum.22 = bf16[2,112]{1,0:T(2,128)(2,1)S(1)} all-reduce(bf16[2,112]{1,0:T(2,128)(2,1)S(1)} %copy.13), channel_id=1, replica_groups=mesh['section'=8,'dp'=64] {'section'}, use_global_device_ids=true, to_apply=%region_11.12 | all-reduce | flops 224 | bytes 896 | tf_op jit(solution)/shard_map/psum | solution.py:139
  1030.4 90.8 %all-reduce.5.cloned.1.call-done = bf16[192,3584]{1,0:T(8,128)(2,1)} async-done(((bf16[192,3584]{1,0:T(8,128)(2,1)}), bf16[192,3584]{1,0:T(8,128)(2,1)}) %all-reduce.5.cloned.1.call-update) | async-done | bytes 1376272 | tf_op jit(solution)/shard_map/psum | solution.py:138
  1123.0 533.6 %all-reduce.3.cloned.1.call-done = f32[1,128,3584]{2,1,0:T(8,128)} async-done(((f32[1,128,3584]{2,1,0:T(8,128)}), f32[1,128,3584]{2,1,0:T(8,128)}) %all-reduce.3.cloned.1.call-update) | async-done | bytes 1835024 | tf_op jit(solution)/shard_map/psum | solution.py:135
  1656.6 286.1 %reduce-scatter.5.cloned.1.call-done = f32[112,128]{1,0:T(8,128)} async-done(((f32[7168,128]{1,0:T(8,128)}), f32[112,128]{1,0:T(8,128)}) %reduce-scatter.5.cloned.1.call-update) | async-done | bytes 57360 | tf_op jit(solution)/shard_map/reduce_scatter | solution.py:132
  (499 shorter events, 251.5 us)
Async XLA Ops:
  7.2 90.2 %copy-start.5 = (f32[2,7168]{1,0:T(2,128)S(1)}, f32[2,7168]{1,0:T(2,128)}, u32[]{:S(2)}) copy-start(f32[2,7168]{1,0:T(2,128)} %param.13) | copy-start | bytes 172036
  7.2 124.7 %all-gather.4.cloned.1.call-start = ((), (), s32[]{:S(2)}) async-start(), calls=%async_computation.5 | async-start | bytes 1863680 | tf_op jit(solution)/shard_map/all_gather | solution.py:50
  7.9 996.7 %reduce-scatter.7.cloned.1.call-start = ((), (), s32[]{:S(2)}) async-start(), calls=%async_computation.6 | async-start | bytes 3727360
  138.7 8.4 collective-permute-start
  152.1 7.6 collective-permute-start
  164.6 7.9 collective-permute-start
  177.5 13.3 collective-permute-start
  195.8 13.4 collective-permute-start
  214.2 13.3 collective-permute-start
  232.5 13.4 collective-permute-start
  250.8 13.4 collective-permute-start
  269.2 13.4 collective-permute-start
  287.6 13.4 collective-permute-start
  306.0 13.4 collective-permute-start
  324.4 13.4 collective-permute-start
  342.8 13.4 collective-permute-start
  361.2 13.4 collective-permute-start
  379.5 13.7 collective-permute-start
  401.0 14.2 collective-permute-start.1
  406.9 8.4 copy-start.3
  421.9 14.8 collective-permute-start.1
  423.8 4.8 copy-start.2
  429.9 6.7 copy-start.3
  443.3 16.8 collective-permute-start.1
  445.2 4.8 copy-start.2
  451.3 8.8 copy-start.3
  466.6 14.4 collective-permute-start.1
  468.6 4.8 copy-start.2
  474.7 6.4 copy-start.3
  487.7 12.9 collective-permute-start.1
  489.6 4.8 copy-start.2
  495.7 4.9 copy-start.3
  507.2 13.3 collective-permute-start.1
  509.1 4.8 copy-start.2
  515.2 5.3 copy-start.3
  527.1 13.6 collective-permute-start.1
  529.0 4.8 copy-start.2
  535.1 5.6 copy-start.3
  547.3 13.6 collective-permute-start.1
  549.3 4.8 copy-start.2
  555.3 5.6 copy-start.3
  567.5 13.6 collective-permute-start.1
  569.5 4.8 copy-start.2
  575.6 5.6 copy-start.3
  587.8 13.6 collective-permute-start.1
  595.8 5.6 copy-start.3
  608.0 13.6 collective-permute-start.1
  609.9 4.8 copy-start.2
  616.0 5.6 copy-start.3
  628.2 13.6 collective-permute-start.1
  630.2 4.8 copy-start.2
  636.2 5.6 copy-start.3
  648.5 13.6 collective-permute-start.1
  650.4 4.8 copy-start.2
  656.5 5.6 copy-start.3
  668.7 13.6 collective-permute-start.1
  670.6 4.8 copy-start.2
  676.7 5.6 copy-start.3
  688.9 13.6 collective-permute-start.1
  690.8 4.8 copy-start.2
  696.9 5.6 copy-start.3
  705.8 415.5 %all-reduce.5.cloned.1.call-start = ((), (), s32[]{:S(2)}) async-start(), calls=%async_computation.4 | async-start | bytes 2752512 | tf_op jit(solution)/shard_map/psum | solution.py:138
  706.5 950.1 %all-reduce.3.cloned.1.call-start = ((), (), s32[]{:S(2)}) async-start(), calls=%async_computation.3 | async-start | bytes 3670016 | tf_op jit(solution)/shard_map/psum | solution.py:135
  707.1 1235.6 %reduce-scatter.5.cloned.1.call-start = ((), (), s32[]{:S(2)}) async-start(), calls=%async_computation.2 | async-start | bytes 3727360 | tf_op jit(solution)/shard_map/reduce_scatter | solution.py:132
  (47 other events, 127.7 us)
Sparse Core Ops, SparseCore 0:
  10.2 121.6 all-gather.3
  705.9 298.6 reduce-scatter.6
  1007.8 113.3 all-reduce.4
  1124.6 531.9 all-reduce.2
  1660.0 282.5 reduce-scatter.4
where the time goes:
time: 1960 us; the launch traced here: 1950 us
  waiting for transfers between devices  1380 us (70%)
  starting transfers between devices  167 us (9%)
  matrix products  132 us (7%)
  blocking collectives  113 us (6%)
  local copies, waits for them, and re-layouts  78.5 us (4%)
  other arithmetic  64.9 us (3%)
    psum x1, waiting for transfers between devices, per_device(): grad_b_sum = lax.psum(grad_b, 'dp')  534 us
    unnamed x6, waiting for transfers between devices  299 us
    reduce_scatter x1, waiting for transfers between devices, per_device(): lax.psum_scatter(grad_a, 'dp', scatter_dimension=0, tiled=True)  286 us
    ppermute x30, starting transfers between devices, from_behind(): return lax.ppermute(block, axis, route)  166 us
    ppermute x30, waiting for transfers between devices, from_behind(): return lax.ppermute(block, axis, route)  137 us
    dot_general x60, matrix products, contract(): lax.dot_general(left_op, right_op, (((left_dim,), (right_dim,)), ((), ())...  112 us
    psum x1, waiting for transfers between devices, per_device(): lax.psum(embed_terms.astype(jnp.bfloat16), 'section').astype(jnp.float32)  90.8 us
    all_gather x1, blocking collectives, per_device(): lax.all_gather(adapter_b[0], 'dp', axis=1, tiled=True)  88.9 us
  transfers between devices with their start and end apart: 35, of which 35 were waited for; matrix products, arithmetic and copies ran while one was open for 5% of the time, Pallas kernels for 0%

commit v1 on v0

--- a/solution.py
+++ b/solution.py
@@ -135,7 +135,9 @@
     grad_b_sum = lax.psum(grad_b, "dp")
     embed_terms = term_keep.reshape(-1, model_width).astype(jnp.float32)
     embed_sum, gain_sum = (
-        lax.psum(embed_terms.astype(jnp.bfloat16), "section").astype(jnp.float32),
+        jnp.sum(lax.all_gather(embed_terms.astype(jnp.bfloat16), "section"), axis=0).astype(
+            jnp.float32
+        ),
         lax.psum(gain_part.astype(jnp.bfloat16), "section").astype(jnp.float32),
     )
     column_count = model_width // sections

time: 1960 us -> 2040 us (1.041)
  waiting for transfers between devices: 1380 us -> 1470 us
    all_gather x0 -> x1, waiting for transfers between devices: none -> 190 us  [per_device(): lax.all_gather(embed_terms.astype(jnp.bfloat16), 'section')]
    psum x1 -> x0, waiting for transfers between devices: 90.8 us -> none  [per_device(): lax.psum(embed_terms.astype(jnp.bfloat16), 'section').astype(jnp.float32)]
where the time goes in v1:
time: 2040 us
  waiting for transfers between devices  1470 us (72%)
  starting transfers between devices  167 us (8%)
  matrix products  133 us (7%)
  blocking collectives  112 us (5%)
  other arithmetic  69.2 us (3%)
  local copies, waits for them, and re-layouts  67.9 us (3%)
    psum x1, waiting for transfers between devices, per_device(): grad_b_sum = lax.psum(grad_b, 'dp')  523 us
    unnamed x6, waiting for transfers between devices  302 us
    reduce_scatter x1, waiting for transfers between devices, per_device(): lax.psum_scatter(grad_a, 'dp', scatter_dimension=0, tiled=True)  286 us
    all_gather x1, waiting for transfers between devices, per_device(): lax.all_gather(embed_terms.astype(jnp.bfloat16), 'section')  190 us
    ppermute x30, starting transfers between devices, from_behind(): return lax.ppermute(block, axis, route)  166 us
    ppermute x30, waiting for transfers between devices, from_behind(): return lax.ppermute(block, axis, route)  135 us
    dot_general x60, matrix products, contract(): lax.dot_general(left_op, right_op, (((left_dim,), (right_dim,)), ((), ())...  114 us
    all_gather x1, blocking collectives, per_device(): lax.all_gather(adapter_b[0], 'dp', axis=1, tiled=True)  88.8 us
  transfers between devices with their start and end apart: 35, of which 35 were waited for; matrix products, arithmetic and copies ran while one was open for 5% of the time, Pallas kernels for 0%

profile of v1, /device:TPU:2, one launch (start us, length us, event | category | flops | bytes accessed | tf_op | source)
XLA Modules:
  0.0 2035.9 jit_solution(14215943740278383939)
XLA Ops:
  8.0 88.8 %all-gather.1 = bf16[1,128,3584]{1,2,0:T(8,128)(2,1)S(1)} all-gather(bf16[1,128,56]{1,2,0:T(8,128)(2,1)} %param.12), channel_id=3, replica_groups=mesh['section'=8,'dp'=64] {'dp'}, dimensions={2}, use_global_device_ids=true | all-gather | bytes 931840 | tf_op jit(solution)/shard_map/all_gather | solution.py:51
  97.4 34.4 %all-gather.7.cloned.1.call-done = bf16[1,7168,128]{2,1,0:T(8,128)(2,1)} async-done(((bf16[1,112,128]{2,1,0:T(8,128)(2,1)}), bf16[1,7168,128]{2,1,0:T(8,128)(2,1)}) %all-gather.7.cloned.1.call-update) | async-done | bytes 1835024 | tf_op jit(solution)/shard_map/all_gather | solution.py:50
  133.7 259.4 %while.42 = (s32[]{:T(128)}, bf16[24,3584]{1,0:T(8,128)(2,1)S(1)}, bf16[8,24,3584]{2,1,0:T(8,128)(2,1)}, bf16[8,24,128]{2,1,0:T(8,128)(2,1)}, s32[]{:T(128)}, /*...) while((s32[]{:T(128)}, bf16[24,3584]{1,0:T(8,128)(2,1)S(1)}, ...), condition=%wide.region_2.3_spmd, body=%wide.region_0.2_spmd.sunk | while | flops 67958816 | bytes 14632085 | solution.py:90
  138.7 3.4 collective-permute-start
  142.0 5.0 collective-permute-done
  152.0 3.4 collective-permute-start
  155.4 4.2 collective-permute-done
  164.6 5.0 collective-permute-start
  169.6 2.9 collective-permute-done
  177.5 10.4 collective-permute-start
  187.9 2.9 collective-permute-done
  195.8 10.5 collective-permute-start
  214.1 10.4 collective-permute-start
  224.6 2.9 collective-permute-done
  232.4 10.4 collective-permute-start
  250.7 10.5 collective-permute-start
  261.2 2.9 collective-permute-done
  269.1 10.5 collective-permute-start
  279.6 2.9 collective-permute-done
  287.5 10.5 collective-permute-start
  298.0 2.9 collective-permute-done
  305.9 10.5 collective-permute-start
  316.4 2.9 collective-permute-done
  324.2 10.5 collective-permute-start
  334.8 2.9 collective-permute-done
  342.6 10.5 collective-permute-start
  361.0 10.5 collective-permute-start
  379.4 10.8 collective-permute-start
  394.3 296.4 %while.43 = (s32[]{:T(128)}, bf16[24,3584]{1,0:T(8,128)(2,1)S(1)}, f32[7168,128]{1,0:T(8,128)}, f32[128,3584]{1,0:T(8,128)}, f32[7168]{0:T(1024)S(1)}, /*index=5...) while((s32[]{:T(128)}, bf16[24,3584]{1,0:T(8,128)(2,1)S(1)}, ...), condition=%wide.region_7.8_spmd.clone, body=%wide.region_3.7_spmd.clone.sunk | while | flops 141248544 | bytes 43407176 | solution.py:125
  406.1 8.5 collective-permute-done.1
  422.5 4.9 convolution_add_fusion.5
  428.7 7.7 collective-permute-done.1
  444.2 4.9 convolution_add_fusion.5
  450.4 7.4 collective-permute-done.1
  465.6 4.9 convolution_add_fusion.5
  471.8 4.8 collective-permute-done.1
  484.4 4.9 convolution_add_fusion.5
  490.6 5.1 collective-permute-done.1
  503.5 4.9 convolution_add_fusion.5
  509.7 5.4 collective-permute-done.1
  523.0 4.9 convolution_add_fusion.5
  529.2 5.5 collective-permute-done.1
  542.5 4.9 convolution_add_fusion.5
  548.7 5.4 collective-permute-done.1
  562.0 4.9 convolution_add_fusion.5
  568.2 5.5 collective-permute-done.1
  581.5 4.9 convolution_add_fusion.5
  587.7 5.4 collective-permute-done.1
  601.0 4.9 convolution_add_fusion.5
  607.2 5.5 collective-permute-done.1
  620.5 4.9 convolution_add_fusion.5
  626.7 5.5 collective-permute-done.1
  639.9 4.9 convolution_add_fusion.5
  646.2 5.5 collective-permute-done.1
  659.5 4.9 convolution_add_fusion.5
  665.7 5.5 collective-permute-done.1
  679.0 4.9 convolution_add_fusion.5
  685.2 5.5 collective-permute-done.1
  695.1 299.6 %reduce-scatter.7.cloned.1.call-done = f32[112,2]{1,0:T(8,128)} async-done(((f32[7168,2]{1,0:T(8,128)}), f32[112,2]{1,0:T(8,128)}) %reduce-scatter.7.cloned.1.call-update) | async-done | bytes 912
  995.6 23.6 %psum.15 = bf16[2,112]{1,0:T(2,128)(2,1)S(1)} all-reduce(bf16[2,112]{1,0:T(2,128)(2,1)S(1)} %copy.13), channel_id=1, replica_groups=mesh['section'=8,'dp'=64] {'section'}, use_global_device_ids=true, to_apply=%region_11.12 | all-reduce | flops 224 | bytes 896 | tf_op jit(solution)/shard_map/psum | solution.py:141
  1019.9 190.4 %all-gather.5.cloned.1.call-done = bf16[8,192,3584]{2,1,0:T(8,128)(2,1)} async-done(((bf16[1,192,3584]{2,1,0:T(8,128)(2,1)}), bf16[8,192,3584]{2,1,0:T(8,128)(2,1)}) %all-gather.5.cloned.1.call-update) | async-done | bytes 11010064 | tf_op jit(solution)/shard_map/all_gather | solution.py:138
  1210.3 6.4 reduce_sum.71
  1217.5 523.2 %all-reduce.2.cloned.1.call-done = f32[1,128,3584]{2,1,0:T(8,128)} async-done(((f32[1,128,3584]{2,1,0:T(8,128)}), f32[1,128,3584]{2,1,0:T(8,128)}) %all-reduce.2.cloned.1.call-update) | async-done | bytes 1835024 | tf_op jit(solution)/shard_map/psum | solution.py:135
  1740.7 285.8 %reduce-scatter.5.cloned.1.call-done = f32[112,128]{1,0:T(8,128)} async-done(((f32[7168,128]{1,0:T(8,128)}), f32[112,128]{1,0:T(8,128)}) %reduce-scatter.5.cloned.1.call-update) | async-done | bytes 57360 | tf_op jit(solution)/shard_map/reduce_scatter | solution.py:132
  (470 shorter events, 241.7 us)
Async XLA Ops:
  7.2 90.2 %copy-start.4 = (f32[2,7168]{1,0:T(2,128)S(1)}, f32[2,7168]{1,0:T(2,128)}, u32[]{:S(2)}) copy-start(f32[2,7168]{1,0:T(2,128)} %param.13) | copy-start | bytes 172036
  7.2 124.7 %all-gather.7.cloned.1.call-start = ((), (), s32[]{:S(2)}) async-start(), calls=%async_computation.5 | async-start | bytes 1863680 | tf_op jit(solution)/shard_map/all_gather | solution.py:50
  7.9 986.9 %reduce-scatter.7.cloned.1.call-start = ((), (), s32[]{:S(2)}) async-start(), calls=%async_computation.6 | async-start | bytes 3727360
  138.7 8.4 collective-permute-start
  152.0 7.6 collective-permute-start
  164.6 7.9 collective-permute-start
  177.5 13.3 collective-permute-start
  195.8 13.4 collective-permute-start
  214.1 13.3 collective-permute-start
  232.4 13.3 collective-permute-start
  250.7 13.4 collective-permute-start
  269.1 13.4 collective-permute-start
  287.5 13.4 collective-permute-start
  305.9 13.4 collective-permute-start
  324.2 13.4 collective-permute-start
  342.6 13.4 collective-permute-start
  361.0 13.4 collective-permute-start
  379.4 13.7 collective-permute-start
  400.2 14.5 collective-permute-start.1
  406.1 8.6 copy-start.3
  420.6 15.8 collective-permute-start.1
  422.5 4.9 copy-start.2
  428.7 7.7 copy-start.3
  442.3 15.6 collective-permute-start.1
  444.2 4.9 copy-start.2
  450.4 7.4 copy-start.3
  463.7 12.9 collective-permute-start.1
  465.6 4.9 copy-start.2
  482.5 13.3 collective-permute-start.1
  484.4 4.9 copy-start.2
  490.6 5.1 copy-start.3
  501.6 13.6 collective-permute-start.1
  503.5 4.9 copy-start.2
  509.7 5.5 copy-start.3
  521.1 13.6 collective-permute-start.1
  523.0 4.9 copy-start.2
  529.2 5.5 copy-start.3
  540.6 13.6 collective-permute-start.1
  542.5 4.9 copy-start.2
  548.7 5.5 copy-start.3
  560.0 13.6 collective-permute-start.1
  562.0 4.9 copy-start.2
  568.2 5.5 copy-start.3
  579.6 13.6 collective-permute-start.1
  581.5 4.9 copy-start.2
  587.7 5.5 copy-start.3
  599.0 13.6 collective-permute-start.1
  600.9 4.9 copy-start.2
  607.1 5.5 copy-start.3
  618.5 13.6 collective-permute-start.1
  620.4 4.9 copy-start.2
  626.6 5.5 copy-start.3
  638.0 13.7 collective-permute-start.1
  639.9 4.9 copy-start.2
  646.1 5.5 copy-start.3
  657.6 13.6 collective-permute-start.1
  659.5 4.9 copy-start.2
  665.7 5.5 copy-start.3
  677.1 13.6 collective-permute-start.1
  679.0 4.9 copy-start.2
  685.2 5.5 copy-start.3
  693.2 517.0 %all-gather.5.cloned.1.call-start = ((), (), s32[]{:S(2)}) async-start(), calls=%async_computation.4 | async-start | bytes 12386304 | tf_op jit(solution)/shard_map/all_gather | solution.py:138
  694.0 1046.7 %all-reduce.2.cloned.1.call-start = ((), (), s32[]{:S(2)}) async-start(), calls=%async_computation.3 | async-start | bytes 3670016 | tf_op jit(solution)/shard_map/psum | solution.py:135
  694.5 1332.0 %reduce-scatter.5.cloned.1.call-start = ((), (), s32[]{:S(2)}) async-start(), calls=%async_computation.2 | async-start | bytes 3727360 | tf_op jit(solution)/shard_map/reduce_scatter | solution.py:132
  (32 other events, 102.6 us)
Sparse Core Ops, SparseCore 0:
  10.2 121.6 all-gather.6
  693.3 301.3 reduce-scatter.6
  998.4 211.7 all-gather.4
  1213.9 526.7 all-reduce.1
  1743.9 282.5 reduce-scatter.4
